TPU v7x, 32 devices: a whole 2x2x4 slice. The times are simulated.
32 devices in a mesh: dom: 2 (over y), feat: 4 (over z), tok: 4 (over x, core).
Axes of the slice: x: 2, y: 2, z: 4, core: 2. Of those that a mesh axis runs over, the one named last changes fastest.
Arguments:
- activations: bfloat16 [16384, 14336], P(('dom', 'tok'), 'feat'), parts along dimension 0, may hold values from -6 to 6
- out_grads: bfloat16 [16384, 4096], P(('dom', 'tok'), 'feat'), parts along dimension 0, may hold values from -6 to 6
- proj_in: bfloat16 [64, 14336], P(None, 'feat'), may hold values from -0.046875 to 0.046875
- proj_out: bfloat16 [64, 4096], P(None, 'feat'), may hold values from -0.09375 to 0.09375
- block_example: int32 [128], P(('dom', 'tok')), parts along dimension 0, may hold values from 0 to 31, as said below
- block_fill: int32 [128], P(('dom', 'tok')), parts along dimension 0, may hold values from 1 to 128
Outputs:
- features: float32 [64, 4096], P(('dom', 'tok'), 'feat'), parts along dimension 0
There are 2 independent parts, one for each index of `dom`. A program takes and returns all parts, laid end to end along the dimension named above; an argument that names none is the same for every part. Nothing has to cross between parts.
Inputs may be any that keep to these rules, and one draw needn't show every extreme that they name: `block_example`: values are example numbers; example e's home is index e // 8 of tok. Among the blocks held by one index of tok, at most 8 belong to examples of any one home, and some home has exactly 8 of them in every draw.
All inputs are finite; a program needn't handle non-finite values.
Results may differ from a plain program's by a relative error of at most 0.0003.
Values sent between devices are 32-bit elements; how exact they have to be, the bound alone decides.
A program may use at most 64 MiB of HBM per device.

v0:
```python
import jax
import jax.numpy as jnp
from jax import lax
from jax.sharding import PartitionSpec as P

R = 64
BLK = 128
EX_DEV = 8


feature_scale = 0.088388


def shards(activations, out_grads, proj_in, proj_out, block_example, block_fill):
    tok_rows = activations.shape[0]
    blocks_dev = tok_rows // BLK
    home_count = lax.axis_size("tok")
    slots = jnp.arange(tok_rows, dtype=jnp.int32)
    block_of = slots // BLK
    block_match = block_of[:, None] == jnp.arange(blocks_dev, dtype=jnp.int32)[None, :]
    fill_row = jnp.sum(jnp.where(block_match, block_fill[None, :], 0), axis=1)
    live = (slots % BLK < fill_row).astype(jnp.float32)
    contract = (((1,), (1,)), ((), ()))
    side_in = lax.dot_general(activations, proj_in, contract, preferred_element_type=jnp.float32)
    side_out = lax.dot_general(out_grads, proj_out, contract, preferred_element_type=jnp.float32)
    paired = jnp.concatenate([side_out, side_in], axis=1) * live[:, None]
    share = lax.psum_scatter(paired, "feat", scatter_dimension=0, tiled=True)
    share_rows = share.shape[0]
    first = lax.axis_index("feat") * share_rows
    share_block = (first + jnp.arange(share_rows, dtype=jnp.int32)) // BLK
    share_match = share_block[:, None] == jnp.arange(blocks_dev, dtype=jnp.int32)[None, :]
    example = jnp.sum(jnp.where(share_match, block_example[None, :], 0), axis=1)
    all_examples = EX_DEV * home_count
    member = (example[:, None] == jnp.arange(all_examples, dtype=jnp.int32)[None, :]).astype(
        jnp.float32
    )
    outer = (share[:, :R, None] * share[:, None, R:]).reshape(share_rows, R * R)
    home_rows = lax.psum_scatter(
        jnp.dot(
            member.T, outer, precision=lax.Precision.HIGHEST, preferred_element_type=jnp.float32
        )
        * feature_scale,
        "tok",
        scatter_dimension=0,
        tiled=True,
    )
    return lax.psum_scatter(home_rows, "feat", scatter_dimension=1, tiled=True)


def solution(mesh):
    in_specs = (
        P(("dom", "tok"), "feat"),
        P(("dom", "tok"), "feat"),
        P(None, "feat"),
        P(None, "feat"),
        P(("dom", "tok")),
        P(("dom", "tok")),
    )
    out_specs = P(("dom", "tok"), "feat")
    return jax.shard_map(shards, mesh=mesh, in_specs=in_specs, out_specs=out_specs, check_vma=False)
```

profile of v0, /device:TPU:0, one launch (start us, length us, event | category | flops | bytes accessed | tf_op | source)
XLA Modules:
  0.0 105.7 jit_solution(3706889441606888513)
XLA Ops:
  6.5 0.0 copy-start
  6.5 0.0 reduce-scatter.4.cloned.1.call-start
  6.5 0.8 select_reduce_fusion
  7.4 0.2 copy-done
  7.6 0.0 copy-start.1
  7.6 9.8 %fusion.15 = f32[2048,64]{0,1:T(8,128)S(1)} fusion(bf16[2048,3584]{1,0:T(8,128)(2,1)} %param.6, bf16[64,3584]{1,0:T(8,128)(2,1)S(1)} %copy-done), kind=kOutput, calls=%fused_computation.33 | convolution fusion | flops 939524096 | bytes 15663104 | tf_op jit(solution)/shard_map/dot_general | solution.py:24
  17.4 0.0 copy-done.1
  17.4 0.0 copy-done.2
  17.4 0.0 copy-start.3
  17.4 1.4 %fusion.14 = f32[2048,64]{0,1:T(8,128)S(1)} fusion(bf16[2048,1024]{1,0:T(8,128)(2,1)S(1)} %copy-done.1, bf16[64,1024]{1,0:T(8,128)(2,1)S(1)} %copy-done.2), kind=kOutput, calls=%fused_computation.32 | convolution fusion | flops 268435456 | bytes 4849664 | tf_op jit(solution)/shard_map/dot_general | solution.py:25
  18.8 1.1 %maximum_multiply_fusion = f32[2048,128]{0,1:T(8,128)} fusion(f32[2048,64]{0,1:T(8,128)S(1)} %fusion.15, f32[2048,64]{0,1:T(8,128)S(1)} %fusion.14, f32[2048]{0:T(1024)S(1)} %fusion.9), kind=kLoop, calls=%fused_computation.2 | loop fusion | flops 524288 | bytes 2105344 | tf_op jit(solution)/shard_map/mul | solution.py:26
  19.9 0.0 reduce-scatter.4.cloned.1.call-update
  19.9 0.0 reduce-scatter.6.cloned.1.call-start
  20.0 0.0 copy-done.3
  20.0 0.1 select_reduce_fusion.1
  20.1 29.8 %reduce-scatter.4.cloned.1.call-done = f32[512,128]{0,1:T(8,128)} async-done(((f32[2048,128]{0,1:T(8,128)}), f32[512,128]{0,1:T(8,128)}) %reduce-scatter.4.cloned.1.call-update) | async-done | bytes 262160 | tf_op jit(solution)/shard_map/reduce_scatter | solution.py:27
  49.9 1.0 fusion.13
  50.9 1.1 %broadcast_multiply_fusion = f32[512,64,64]{0,2,1:T(8,128)S(1)} fusion(f32[512,64]{0,1:T(8,128)S(1)} %get-tuple-element.6, f32[512,64]{0,1:T(8,128)S(1)} %get-tuple-element.5), kind=kLoop, calls=%fused_computation.1 | loop fusion | flops 2097152 | bytes 8650752 | tf_op jit(solution)/shard_map/mul | solution.py:37
  52.0 5.1 %convolution_multiply_fusion = f32[32,4096]{1,0:T(8,128)} fusion(f32[512,4096]{0,1:T(8,128)S(1)} %bitcast.6, s32[512]{0:T(512)S(1)} %select_reduce_fusion.1), kind=kOutput, calls=%fused_computation | convolution fusion | flops 805470208 | bytes 8914944 | tf_op jit(solution)/shard_map/dot_general | solution.py:39
  57.2 0.0 reduce-scatter.6.cloned.1.call-update
  57.2 0.0 reduce-scatter.8.cloned.1.call-start
  57.2 20.4 %reduce-scatter.6.cloned.1.call-done = f32[8,4096]{1,0:T(8,128)} async-done(((f32[32,4096]{1,0:T(8,128)}), f32[8,4096]{1,0:T(8,128)}) %reduce-scatter.6.cloned.1.call-update) | async-done | bytes 131088 | tf_op jit(solution)/shard_map/reduce_scatter | solution.py:38
  77.7 0.0 reduce-scatter.8.cloned.1.call-update
  77.7 21.5 %reduce-scatter.8.cloned.1.call-done = f32[8,1024]{1,0:T(8,128)} async-done(((f32[8,4096]{1,0:T(8,128)}), f32[8,1024]{1,0:T(8,128)}) %reduce-scatter.8.cloned.1.call-update) | async-done | bytes 32784 | tf_op jit(solution)/shard_map/reduce_scatter | solution.py:47
  (4 shorter events, 0.0 us)
Async XLA Ops:
  6.5 1.0 copy-start
  6.5 43.4 %reduce-scatter.4.cloned.1.call-start = ((), (), s32[]{:S(2)}) async-start(), calls=%async_computation.3 | async-start | bytes 1310720 | tf_op jit(solution)/shard_map/reduce_scatter | solution.py:27
  7.6 9.8 %copy-start.1 = (bf16[2048,1024]{1,0:T(8,128)(2,1)S(1)}, bf16[2048,1024]{1,0:T(8,128)(2,1)}, u32[]{:S(2)}) copy-start(bf16[2048,1024]{1,0:T(8,128)(2,1)} %param.7) | copy-start | bytes 12582916
  7.6 9.8 %copy-start.2 = (bf16[64,1024]{1,0:T(8,128)(2,1)S(1)}, bf16[64,1024]{1,0:T(8,128)(2,1)}, u32[]{:S(2)}) copy-start(bf16[64,1024]{1,0:T(8,128)(2,1)} %param.9) | copy-start | bytes 393220
  17.4 2.6 %copy-start.3 = (s32[16]{0:T(128)S(1)}, s32[16]{0:T(128)}, u32[]{:S(2)}) copy-start(s32[16]{0:T(128)} %param.10) | copy-start | bytes 196
  19.9 57.7 %reduce-scatter.6.cloned.1.call-start = ((), (), s32[]{:S(2)}) async-start(), calls=%async_computation.4 | async-start | bytes 655360 | tf_op jit(solution)/shard_map/reduce_scatter | solution.py:38
  57.2 41.9 %reduce-scatter.8.cloned.1.call-start = ((), (), s32[]{:S(2)}) async-start(), calls=%async_computation.5 | async-start | bytes 163840 | tf_op jit(solution)/shard_map/reduce_scatter | solution.py:47
Sparse Core Ops, SparseCore 0:
  20.1 29.8 reduce-scatter.3
  57.3 20.2 reduce-scatter.5
  79.9 19.1 reduce-scatter.7
where the time goes:
time: 106 us
  waiting for transfers between devices  71.7 us (68%)
  matrix products  16.4 us (15%)
  between operations  13.2 us (12%)
  other arithmetic  3.11 us (3%)
  local copies, waits for them, and re-layouts  1.21 us (1%)
    reduce_scatter x1, waiting for transfers between devices, shards(): share = lax.psum_scatter(paired, 'feat', scatter_dimension=0, tiled=True)  29.8 us
    reduce_scatter x1, waiting for transfers between devices, shards(): return lax.psum_scatter(home_rows, 'feat', scatter_dimension=1, tiled=True)  21.5 us
    reduce_scatter x1, waiting for transfers between devices, shards(): lax.psum_scatter(jnp.dot(member.T, outer, precision=lax.Precision.HIGHEST...  20.4 us
    dot_general x1, matrix products, shards(): lax.dot_general(activations, proj_in, contract, preferred_element_type=jn...  9.82 us
    dot_general x1, matrix products, shards(): jnp.dot(member.T, outer, precision=lax.Precision.HIGHEST, preferred_eleme...  5.15 us
  transfers between devices with their start and end apart: 3, of which 3 were waited for; matrix products, arithmetic and copies ran while one was open for 0% of the time, Pallas kernels for 0%

commit v1 on v0

v1 whole, which is shorter than its diff:
```python
import functools

import jax
import jax.numpy as jnp
from jax import lax
from jax.experimental import pallas as pl
from jax.experimental.pallas import tpu as pltpu
from jax.sharding import PartitionSpec as P

R = 64
BLK = 128
EX_DEV = 8
LANES = 128
NEAR_LAG = 2
FAR_LAG = 4
MESH = pl.DeviceIdType.MESH

feature_scale = 0.088388


def kernel(
    feats, toks, pieces,
    act_ref, grad_ref, pin_ref, pout_ref, example_ref, fill_ref,
    out_ref,
    act_buf, grad_buf, win, wout, own, inbox, square, gath, ids, acc, fin,
    load_sem, weight_sem, send_sem, recv_sem, block_send, block_recv,
    id_send, id_recv, fin_send, fin_recv,
):
    half = pieces * BLK
    f = lax.axis_index("feat")
    me = lax.axis_index("tok")
    part_rows = fin.shape[1]
    near = jnp.where(f < feats // 2, 0, 1)
    far = 1 - near
    is_end = jnp.logical_or(f == 0, f == feats - 1)
    is_mid = jnp.logical_not(is_end)

    def loads(p):
        copies = []
        for d in range(2):
            rows = pl.ds(pl.multiple_of((1 - d) * half + p * BLK, BLK), BLK)
            slot = pl.ds(d * BLK, BLK)
            copies.append(pltpu.make_async_copy(
                act_ref.at[rows], act_buf.at[p, slot], load_sem.at[p, 2 * d]))
            copies.append(pltpu.make_async_copy(
                grad_ref.at[rows], grad_buf.at[p, slot], load_sem.at[p, 2 * d + 1]))
        return copies

    win[...] = jnp.zeros_like(win)
    wout[...] = jnp.zeros_like(wout)
    weights = [
        pltpu.make_async_copy(pin_ref, win.at[pl.ds(R, R)], weight_sem.at[0]),
        pltpu.make_async_copy(pout_ref, wout.at[pl.ds(0, R)], weight_sem.at[1]),
    ]
    for copy in weights:
        copy.start()

    @pl.loop(0, pieces)
    def _(p):
        for copy in loads(p):
            copy.start()

    barrier = pltpu.get_barrier_semaphore()
    for j in range(1, feats):
        pl.semaphore_signal(
            barrier, inc=1, device_id={"feat": lax.rem(f + j, feats)}, device_id_type=MESH)
    for j in range(1, toks):
        pl.semaphore_signal(
            barrier, inc=1, device_id={"tok": lax.rem(me + j, toks)}, device_id_type=MESH)

    acc[...] = jnp.zeros_like(acc)
    for b in range(2 * pieces):
        ids[me, b] = jnp.full((LANES,), example_ref[b], jnp.int32).astype(jnp.float32)
    for copy in weights:
        copy.wait()
    pl.semaphore_wait(barrier, feats - 1 + toks - 1)

    def id_copy(j):
        return pltpu.make_async_remote_copy(
            src_ref=ids.at[me], dst_ref=ids.at[me],
            send_sem=id_send.at[j - 1], recv_sem=id_recv.at[me],
            device_id={"tok": lax.rem(me + j, toks)}, device_id_type=MESH)

    def id_arrival(t):
        return pltpu.make_async_remote_copy(
            src_ref=ids.at[me], dst_ref=ids.at[t],
            send_sem=id_send.at[0], recv_sem=id_recv.at[t],
            device_id={"tok": t}, device_id_type=MESH)

    def hop(d, p):
        return pltpu.make_async_remote_copy(
            src_ref=own.at[d, p], dst_ref=inbox.at[d, p],
            send_sem=send_sem.at[d, p], recv_sem=recv_sem.at[d, p],
            device_id={"feat": lax.rem(f + 1 - 2 * d + feats, feats)}, device_id_type=MESH)

    def block_copy(p, j):
        return pltpu.make_async_remote_copy(
            src_ref=gath.at[me, p], dst_ref=gath.at[me, p],
            send_sem=block_send.at[p, j - 1], recv_sem=block_recv.at[me, p],
            device_id={"tok": lax.rem(me + j, toks)}, device_id_type=MESH)

    def block_arrival(t, p):
        return pltpu.make_async_remote_copy(
            src_ref=gath.at[me, p], dst_ref=gath.at[t, p],
            send_sem=block_send.at[p, 0], recv_sem=block_recv.at[t, p],
            device_id={"tok": t}, device_id_type=MESH)

    @pl.when(is_end)
    def _():
        for j in range(1, toks):
            id_copy(j).start()

    contract = (((1,), (1,)), ((), ()))

    def project(p):
        for copy in loads(p):
            copy.wait()
        both = lax.dot_general(
            act_buf[p], win[...], contract, preferred_element_type=jnp.float32)
        both += lax.dot_general(
            grad_buf[p], wout[...], contract, preferred_element_type=jnp.float32)
        own[0, p] = both[:BLK]
        own[1, p] = both[BLK:]

    def forward(d, p):
        hop(d, p).wait_recv()
        own[d, p] += inbox[d, p]
        hop(d, p).start()

    @pl.loop(0, pieces + FAR_LAG)
    def _(step):
        @pl.when(step < pieces)
        def _():
            project(step)

            @pl.when(is_end)
            def _():
                hop(near, step).start()

        @pl.when(jnp.logical_and(is_mid, jnp.logical_and(step >= NEAR_LAG, step < pieces + NEAR_LAG)))
        def _():
            forward(near, step - NEAR_LAG)

        @pl.when(jnp.logical_and(is_mid, step >= FAR_LAG))
        def _():
            forward(far, step - FAR_LAG)

    lane = lax.broadcasted_iota(jnp.int32, (BLK, LANES), 1)
    row = lax.broadcasted_iota(jnp.int32, (BLK, LANES), 0)
    half_lane = lax.broadcasted_iota(jnp.int32, (R // 2, LANES), 1)
    home_example = (
        lax.broadcasted_iota(jnp.int32, (EX_DEV, LANES), 0) + me * EX_DEV
    ).astype(jnp.float32)

    def outer(p):
        hop(far, p).wait_recv()
        fill = fill_ref[p + (1 - far) * pieces]
        sides = jnp.where(row < fill, own[far, p] + inbox[far, p], 0.0)
        twice = jnp.where(lane < R, pltpu.roll(sides, R, 1), sides)
        square[...] = lax.dot_general(
            sides, twice, (((0,), (0,)), ((), ())),
            precision=lax.Precision.HIGHEST, preferred_element_type=jnp.float32)[:R]
        even = square[pl.ds(0, R // 2, stride=2), :]
        odd = square[pl.ds(1, R // 2, stride=2), :]
        gath[me, p] = jnp.where(half_lane < R, even, odd)
        for j in range(1, toks):
            block_copy(p, j).start()

    def gather(p):
        for j in range(toks):
            t = lax.rem(me + j, toks)
            if j:
                block_arrival(t, p).wait_recv()
            named = ids[t, pl.ds(p + (1 - far) * pieces, 1), :]
            member = jnp.where(home_example == named, 1.0, 0.0)
            acc[...] += gath[t, p][:, None, :] * member[None]

    def fin_copy(j):
        target = lax.rem(f + j, feats)
        return pltpu.make_async_remote_copy(
            src_ref=acc.at[pl.ds(target * part_rows, part_rows)], dst_ref=fin.at[far],
            send_sem=fin_send.at[j - 1], recv_sem=fin_recv.at[far],
            device_id={"feat": target}, device_id_type=MESH)

    def fin_arrival(slot):
        return pltpu.make_async_remote_copy(
            src_ref=acc.at[pl.ds(0, part_rows)], dst_ref=fin.at[slot],
            send_sem=fin_send.at[0], recv_sem=fin_recv.at[slot],
            device_id={"feat": lax.rem(f + 1, feats)}, device_id_type=MESH)

    @pl.when(is_end)
    def _():
        for j in range(1, toks):
            id_arrival(lax.rem(me + j, toks)).wait_recv()

        @pl.loop(0, pieces + 1)
        def _(p):
            @pl.when(p < pieces)
            def _():
                outer(p)

            @pl.when(p >= 1)
            def _():
                gather(p - 1)

        acc[...] = acc[...] * feature_scale
        for j in range(1, feats):
            fin_copy(j).start()
        fin[far] = acc[pl.ds(f * part_rows, part_rows)]
        fin_arrival(near).wait_recv()

    @pl.when(is_mid)
    def _():
        fin_arrival(0).wait_recv()
        fin_arrival(1).wait_recv()

    for r in range(part_rows):
        out_ref[:, r * LANES:(r + 1) * LANES] = fin[0, r] + fin[1, r]

    @pl.loop(0, pieces)
    def _(p):
        hop(near, p).wait_send()

        @pl.when(is_mid)
        def _():
            hop(far, p).wait_send()

        @pl.when(is_end)
        def _():
            for j in range(1, toks):
                block_copy(p, j).wait_send()

    @pl.when(is_end)
    def _():
        for j in range(1, toks):
            id_copy(j).wait_send()
        for j in range(1, feats):
            fin_copy(j).wait_send()


def shards(feats, toks, activations, out_grads, proj_in, proj_out, block_example, block_fill):
    rows, in_columns = activations.shape
    out_columns = out_grads.shape[1]
    pieces = rows // (2 * BLK)
    out_rows = R * R // LANES
    hbm = pl.BlockSpec(memory_space=pl.ANY)
    smem = pl.BlockSpec(memory_space=pltpu.SMEM)
    dma = pltpu.SemaphoreType.DMA
    return pl.pallas_call(
        functools.partial(kernel, feats, toks, pieces),
        out_shape=jax.ShapeDtypeStruct((EX_DEV, R * R // feats), jnp.float32),
        in_specs=[hbm, hbm, hbm, hbm, smem, smem],
        out_specs=pl.BlockSpec(memory_space=pltpu.VMEM),
        scratch_shapes=[
            pltpu.VMEM((pieces, 2 * BLK, in_columns), jnp.bfloat16),
            pltpu.VMEM((pieces, 2 * BLK, out_columns), jnp.bfloat16),
            pltpu.VMEM((LANES, in_columns), jnp.bfloat16),
            pltpu.VMEM((LANES, out_columns), jnp.bfloat16),
            pltpu.VMEM((2, pieces, BLK, LANES), jnp.float32),
            pltpu.VMEM((2, pieces, BLK, LANES), jnp.float32),
            pltpu.VMEM((R, LANES), jnp.float32),
            pltpu.VMEM((toks, pieces, out_rows, LANES), jnp.float32),
            pltpu.VMEM((toks, 2 * pieces, LANES), jnp.float32),
            pltpu.VMEM((out_rows, EX_DEV, LANES), jnp.float32),
            pltpu.VMEM((2, out_rows // feats, EX_DEV, LANES), jnp.float32),
            dma((pieces, 4)),
            dma((2,)),
            dma((2, pieces)),
            dma((2, pieces)),
            dma((pieces, toks - 1)),
            dma((toks, pieces)),
            dma((toks - 1,)),
            dma((toks,)),
            dma((feats - 1,)),
            dma((2,)),
        ],
        compiler_params=pltpu.CompilerParams(
            collective_id=0, has_side_effects=True, vmem_limit_bytes=48 * 2**20
        ),
        cost_estimate=pl.CostEstimate(
            flops=2 * rows * R * (in_columns + out_columns),
            bytes_accessed=2 * rows * (in_columns + out_columns),
            transcendentals=0,
        ),
    )(activations, out_grads, proj_in, proj_out, block_example, block_fill)


def solution(mesh):
    in_specs = (
        P(("dom", "tok"), "feat"),
        P(("dom", "tok"), "feat"),
        P(None, "feat"),
        P(None, "feat"),
        P(("dom", "tok")),
        P(("dom", "tok")),
    )
    out_specs = P(("dom", "tok"), "feat")
    body = functools.partial(shards, mesh.shape["feat"], mesh.shape["tok"])
    return jax.shard_map(body, mesh=mesh, in_specs=in_specs, out_specs=out_specs, check_vma=False)
```

time: 106 us -> 44.4 us (0.42)
  waiting for transfers between devices: 71.7 us -> 0 us
  Pallas kernels: 0 us -> 38.1 us
  matrix products: 16.4 us -> 0 us
  between operations: 13.2 us -> 0.01 us
  local copies, waits for them, and re-layouts: 1.21 us -> 6.04 us
  other arithmetic: 3.11 us -> 0 us
    reduce_scatter x3 -> x0, waiting for transfers between devices: 71.7 us -> none  [the longest x1 29.8 us: shards(): share = lax.psum_scatter(paired, 'feat', scatter_dimension=0, tiled=True)]
    pallas_call x0 -> x1, Pallas kernels: none -> 38.1 us  [shards(): pl.pallas_call(functools.partial(kernel, feats, toks, pieces), out_shape=...]
    dot_general x3 -> x0, matrix products: 16.4 us -> none  [the longest x1 9.82 us: shards(): lax.dot_general(activations, proj_in, contract, preferred_element_type=jn...]
    unnamed x8 -> x11, local copies, waits for them, and re-layouts: 0.22 us -> 6.04 us
    mul x2 -> x0, other arithmetic: 2.2 us -> none  [the longest x1 1.1 us: shards(): outer = (share[:, :R, None] * share[:, None, R:]).reshape(share_rows, R * R)]
  transfers between devices with their start and end apart: 3 -> 0, of which waited for: 3 -> 0; matrix products, arithmetic and copies ran while one was open for 0% -> 0% of each run, Pallas kernels for 0% -> 0%
where the time goes in v1:
time: 44.4 us; the launch traced here: 44.2 us
  Pallas kernels  38.1 us (86%)
  local copies, waits for them, and re-layouts  6.04 us (14%)
    pallas_call x1, Pallas kernels, shards(): pl.pallas_call(functools.partial(kernel, feats, toks, pieces), out_shape=...  38.1 us
    unnamed x11, local copies, waits for them, and re-layouts  6.04 us

profile of v1, /device:TPU:0, one launch (start us, length us, event | category | flops | bytes accessed | tf_op | source)
XLA Modules:
  0.0 44.2 jit_solution(13610530489851302837)
XLA Ops:
  0.0 0.0 copy-start
  0.0 2.2 %copy-done = bf16[2048,1024]{1,0:T(8,128)(2,1)S(1)} copy-done((bf16[2048,1024]{1,0:T(8,128)(2,1)S(1)}, bf16[2048,1024]{1,0:T(8,128)(2,1)}, u32[]{:S(2)}) %copy-start) | copy-done | bytes 4194328
  2.2 0.0 copy-start.1
  2.2 1.0 %copy-done.1 = bf16[64,3584]{1,0:T(8,128)(2,1)S(1)} copy-done((bf16[64,3584]{1,0:T(8,128)(2,1)S(1)}, bf16[64,3584]{1,0:T(8,128)(2,1)}, u32[]{:S(2)}) %copy-start.1) | copy-done | bytes 458776
  3.2 0.0 copy-start.2
  3.2 0.9 %copy-done.2 = bf16[64,1024]{1,0:T(8,128)(2,1)S(1)} copy-done((bf16[64,1024]{1,0:T(8,128)(2,1)S(1)}, bf16[64,1024]{1,0:T(8,128)(2,1)}, u32[]{:S(2)}) %copy-start.2) | copy-done | bytes 131096
  4.1 0.0 copy-start.3
  4.1 0.7 %copy-done.3 = s32[16]{0:T(128)S(1)} copy-done((s32[16]{0:T(128)S(1)}, s32[16]{0:T(128)}, u32[]{:S(2)}) %copy-start.3) | copy-done | bytes 88
  4.8 0.0 copy-start.4
  4.8 0.7 %copy-done.4 = s32[16]{0:T(128)S(1)} copy-done((s32[16]{0:T(128)S(1)}, s32[16]{0:T(128)}, u32[]{:S(2)}) %copy-start.4) | copy-done | bytes 88
  5.4 38.1 %shard_map.64 = f32[8,1024]{1,0:T(8,128)S(1)} custom-call(bf16[2048,3584]{1,0:T(8,128)(2,1)} %act_ref.1, bf16[2048,1024]{1,0:T(8,128)(2,1)S(1)} %copy-done, bf16[64,3584]{1,0:T(8,128)(2,1)S(1)} %copy-done.1, bf16[64,1024]{1,0:T(8,128)(2,1)S(1)} %copy-done.2, s32[16]{0:T(128)S(1)} %copy-done.3, s32[16]{0:T(128)S(1)} %copy-done.4), custom_call_target="tpu_custom_call" | custom-call | flops 1207959552 | bytes 18874368 | tf_op jit(solution)/shard_map/pallas_call | solution.py:249
  43.5 0.6 %copy.8 = f32[8,1024]{1,0:T(8,128)} copy(f32[8,1024]{1,0:T(8,128)S(1)} %shard_map.64) | data formatting | bytes 65536
Async XLA Ops:
  0.0 2.2 %copy-start = (bf16[2048,1024]{1,0:T(8,128)(2,1)S(1)}, bf16[2048,1024]{1,0:T(8,128)(2,1)}, u32[]{:S(2)}) copy-start(bf16[2048,1024]{1,0:T(8,128)(2,1)} %grad_ref.1) | copy-start | bytes 12582916
  2.2 1.0 %copy-start.1 = (bf16[64,3584]{1,0:T(8,128)(2,1)S(1)}, bf16[64,3584]{1,0:T(8,128)(2,1)}, u32[]{:S(2)}) copy-start(bf16[64,3584]{1,0:T(8,128)(2,1)} %pin_ref.1) | copy-start | bytes 1376260
  3.2 0.9 %copy-start.2 = (bf16[64,1024]{1,0:T(8,128)(2,1)S(1)}, bf16[64,1024]{1,0:T(8,128)(2,1)}, u32[]{:S(2)}) copy-start(bf16[64,1024]{1,0:T(8,128)(2,1)} %pout_ref.1) | copy-start | bytes 393220
  4.1 0.7 %copy-start.3 = (s32[16]{0:T(128)S(1)}, s32[16]{0:T(128)}, u32[]{:S(2)}) copy-start(s32[16]{0:T(128)} %example_ref.1) | copy-start | bytes 196
  4.8 0.7 %copy-start.4 = (s32[16]{0:T(128)S(1)}, s32[16]{0:T(128)}, u32[]{:S(2)}) copy-start(s32[16]{0:T(128)} %fill_ref.1) | copy-start | bytes 196

commit v2 on v1

v2 whole, which is shorter than its diff:
```python
import functools

import jax
import jax.numpy as jnp
from jax import lax
from jax.experimental import pallas as pl
from jax.experimental.pallas import tpu as pltpu
from jax.sharding import PartitionSpec as P

R = 64
BLK = 128
EX_DEV = 8
LANES = 128
NEAR_LAG = 1
FAR_LAG = 4
MID_BLOCKS = 2
MESH = pl.DeviceIdType.MESH

feature_scale = 0.088388


def kernel(
    feats, toks, blocks, end_blocks, mid_blocks,
    act_ref, grad_ref, pin_ref, pout_ref, example_hbm, fill_hbm,
    out_ref,
    example_ref, fill_ref, act_buf, grad_buf, win, wout, own, inbox, square, gath, ids, acc, fin,
    load_sem, weight_sem, send_sem, recv_sem, block_send, block_recv,
    id_send, id_recv, fin_send, fin_recv,
):
    pieces = blocks // 2
    f = lax.axis_index("feat")
    me = lax.axis_index("tok")
    part_rows = fin.shape[1]
    near = jnp.where(f < feats // 2, 0, 1)
    far = 1 - near
    is_end = jnp.logical_or(f == 0, f == feats - 1)
    is_mid = jnp.logical_not(is_end)

    def first_block(owner):
        inner = end_blocks + (owner - 1) * mid_blocks
        return jnp.where(owner <= 0, 0, jnp.where(owner >= feats, blocks, inner))

    lower, upper = first_block(f), first_block(f + 1)
    owned = upper - lower
    rising = f < feats // 2
    near_count = jnp.where(rising, blocks - upper, lower)
    far_count = jnp.where(rising, lower, blocks - upper)

    def block_at(d, p):
        return d * p + (1 - d) * (blocks - 1 - p)

    def loads(p):
        copies = []
        for d in range(2):
            rows = pl.ds(pl.multiple_of(block_at(d, p) * BLK, BLK), BLK)
            slot = pl.ds(d * BLK, BLK)
            copies.append(pltpu.make_async_copy(
                act_ref.at[rows], act_buf.at[p, slot], load_sem.at[p, 2 * d]))
            copies.append(pltpu.make_async_copy(
                grad_ref.at[rows], grad_buf.at[p, slot], load_sem.at[p, 2 * d + 1]))
        return copies

    barrier = pltpu.get_barrier_semaphore()
    for j in range(1, feats):
        pl.semaphore_signal(
            barrier, inc=1, device_id={"feat": lax.rem(f + j, feats)}, device_id_type=MESH)
    for j in range(1, toks):
        pl.semaphore_signal(
            barrier, inc=1, device_id={"tok": lax.rem(me + j, toks)}, device_id_type=MESH)

    win[...] = jnp.zeros_like(win)
    wout[...] = jnp.zeros_like(wout)
    weights = [
        pltpu.make_async_copy(pin_ref, win.at[pl.ds(R, R)], weight_sem.at[0]),
        pltpu.make_async_copy(pout_ref, wout.at[pl.ds(0, R)], weight_sem.at[1]),
        pltpu.make_async_copy(example_hbm, example_ref, weight_sem.at[2]),
        pltpu.make_async_copy(fill_hbm, fill_ref, weight_sem.at[3]),
    ]
    for copy in weights:
        copy.start()

    @pl.loop(0, pieces)
    def _(p):
        for copy in loads(p):
            copy.start()

    for copy in weights:
        copy.wait()
    def id_copy(j):
        return pltpu.make_async_remote_copy(
            src_ref=ids.at[me], dst_ref=ids.at[me],
            send_sem=id_send.at[j - 1], recv_sem=id_recv.at[me],
            device_id={"tok": lax.rem(me + j, toks)}, device_id_type=MESH)

    def id_arrival(t):
        return pltpu.make_async_remote_copy(
            src_ref=ids.at[me], dst_ref=ids.at[t],
            send_sem=id_send.at[0], recv_sem=id_recv.at[t],
            device_id={"tok": t}, device_id_type=MESH)

    def hop(d, b):
        return pltpu.make_async_remote_copy(
            src_ref=own.at[b], dst_ref=inbox.at[d, b],
            send_sem=send_sem.at[b], recv_sem=recv_sem.at[d, b],
            device_id={"feat": lax.rem(f + 1 - 2 * d + feats, feats)}, device_id_type=MESH)

    def block_copy(p, j):
        return pltpu.make_async_remote_copy(
            src_ref=gath.at[me, p], dst_ref=gath.at[me, p],
            send_sem=block_send.at[p, j - 1], recv_sem=block_recv.at[me, p],
            device_id={"tok": lax.rem(me + j, toks)}, device_id_type=MESH)

    def block_arrival(t, p):
        return pltpu.make_async_remote_copy(
            src_ref=gath.at[me, p], dst_ref=gath.at[t, p],
            send_sem=block_send.at[p, 0], recv_sem=block_recv.at[t, p],
            device_id={"tok": t}, device_id_type=MESH)


    contract = (((1,), (1,)), ((), ()))

    def project(p):
        for copy in loads(p):
            copy.wait()
        both = lax.dot_general(
            act_buf[p], win[...], contract, preferred_element_type=jnp.float32)
        both += lax.dot_general(
            grad_buf[p], wout[...], contract, preferred_element_type=jnp.float32)
        own[block_at(0, p)] = both[:BLK]
        own[block_at(1, p)] = both[BLK:]

    def forward(d, q):
        b = block_at(d, q)
        hop(d, b).wait_recv()
        own[b] += inbox[d, b]
        hop(d, b).start()

    @pl.loop(0, blocks + FAR_LAG)
    def _(step):
        @pl.when(step < pieces)
        def _():
            project(step)

        @pl.when(step == 0)
        def _():
            pl.semaphore_wait(barrier, feats - 1 + toks - 1)

        @pl.when(jnp.logical_and(is_end, step < near_count))
        def _():
            hop(near, block_at(near, step)).start()

        @pl.when(jnp.logical_and(
            is_mid, jnp.logical_and(step >= NEAR_LAG, step < near_count + NEAR_LAG)))
        def _():
            forward(near, step - NEAR_LAG)

        @pl.when(jnp.logical_and(
            is_mid, jnp.logical_and(step >= FAR_LAG, step < far_count + FAR_LAG)))
        def _():
            forward(far, step - FAR_LAG)

    acc[...] = jnp.zeros_like(acc)
    for b in range(blocks):
        ids[me, b] = jnp.full((LANES,), example_ref[b], jnp.int32).astype(jnp.float32)
    for j in range(1, toks):
        id_copy(j).start()

    lane = lax.broadcasted_iota(jnp.int32, (BLK, LANES), 1)
    row = lax.broadcasted_iota(jnp.int32, (BLK, LANES), 0)
    half_lane = lax.broadcasted_iota(jnp.int32, (R // 2, LANES), 1)
    home_example = (
        lax.broadcasted_iota(jnp.int32, (EX_DEV, LANES), 0) + me * EX_DEV
    ).astype(jnp.float32)

    def block_of(i):
        return jnp.where(rising, lower + i, upper - 1 - i)

    def outer(i):
        b = block_of(i)

        @pl.when(f > 0)
        def _():
            hop(0, b).wait_recv()
            own[b] += inbox[0, b]

        @pl.when(f < feats - 1)
        def _():
            hop(1, b).wait_recv()
            own[b] += inbox[1, b]

        sides = jnp.where(row < fill_ref[b], own[b], 0.0)
        twice = jnp.where(lane < R, pltpu.roll(sides, R, 1), sides)
        square[...] = lax.dot_general(
            sides, twice, (((0,), (0,)), ((), ())),
            precision=lax.Precision.HIGHEST, preferred_element_type=jnp.float32)[:R]
        even = square[pl.ds(0, R // 2, stride=2), :]
        odd = square[pl.ds(1, R // 2, stride=2), :]
        gath[me, i] = jnp.where(half_lane < R, even, odd)
        for j in range(1, toks):
            block_copy(i, j).start()

    def gather(p):
        for j in range(toks):
            t = lax.rem(me + j, toks)
            if j:
                block_arrival(t, p).wait_recv()
            named = ids[t, pl.ds(block_of(p), 1), :]
            member = jnp.where(home_example == named, 1.0, 0.0)
            acc[...] += gath[t, p][:, None, :] * member[None]

    def fin_copy(j):
        target = lax.rem(f + j, feats)
        return pltpu.make_async_remote_copy(
            src_ref=acc.at[pl.ds(target * part_rows, part_rows)], dst_ref=fin.at[f],
            send_sem=fin_send.at[j - 1], recv_sem=fin_recv.at[f],
            device_id={"feat": target}, device_id_type=MESH)

    def fin_arrival(slot):
        return pltpu.make_async_remote_copy(
            src_ref=acc.at[pl.ds(0, part_rows)], dst_ref=fin.at[slot],
            send_sem=fin_send.at[0], recv_sem=fin_recv.at[slot],
            device_id={"feat": slot}, device_id_type=MESH)

    for j in range(1, toks):
        id_arrival(lax.rem(me + j, toks)).wait_recv()

    @pl.loop(0, owned)
    def _(i):
        outer(i)

    @pl.loop(0, owned)
    def _(i):
        gather(i)

    acc[...] = acc[...] * feature_scale
    for j in range(1, feats):
        fin_copy(j).start()
    fin[f] = acc[pl.ds(f * part_rows, part_rows)]
    for j in range(1, feats):
        fin_arrival(lax.rem(f + j, feats)).wait_recv()

    for r in range(part_rows):
        total = fin[0, r]
        for slot in range(1, feats):
            total += fin[slot, r]
        out_ref[:, r * LANES:(r + 1) * LANES] = total

    @pl.loop(0, near_count)
    def _(q):
        hop(near, block_at(near, q)).wait_send()

    @pl.loop(0, far_count)
    def _(q):
        hop(far, block_at(far, q)).wait_send()

    @pl.loop(0, owned)
    def _(i):
        for j in range(1, toks):
            block_copy(i, j).wait_send()

    for j in range(1, toks):
        id_copy(j).wait_send()
    for j in range(1, feats):
        fin_copy(j).wait_send()


def shards(feats, toks, activations, out_grads, proj_in, proj_out, block_example, block_fill):
    rows, in_columns = activations.shape
    out_columns = out_grads.shape[1]
    blocks = rows // BLK
    pieces = blocks // 2
    mid_blocks = max(0, min(MID_BLOCKS, (blocks - 2) // max(1, feats - 2)))
    end_blocks = (blocks - (feats - 2) * mid_blocks) // 2
    out_rows = R * R // LANES
    hbm = pl.BlockSpec(memory_space=pl.ANY)
    dma = pltpu.SemaphoreType.DMA
    return pl.pallas_call(
        functools.partial(kernel, feats, toks, blocks, end_blocks, mid_blocks),
        out_shape=jax.ShapeDtypeStruct((EX_DEV, R * R // feats), jnp.float32),
        in_specs=[hbm] * 6,
        out_specs=pl.BlockSpec(memory_space=pltpu.VMEM),
        scratch_shapes=[
            pltpu.SMEM(block_example.shape, jnp.int32),
            pltpu.SMEM(block_fill.shape, jnp.int32),
            pltpu.VMEM((pieces, 2 * BLK, in_columns), jnp.bfloat16),
            pltpu.VMEM((pieces, 2 * BLK, out_columns), jnp.bfloat16),
            pltpu.VMEM((LANES, in_columns), jnp.bfloat16),
            pltpu.VMEM((LANES, out_columns), jnp.bfloat16),
            pltpu.VMEM((blocks, BLK, LANES), jnp.float32),
            pltpu.VMEM((2, blocks, BLK, LANES), jnp.float32),
            pltpu.VMEM((R, LANES), jnp.float32),
            pltpu.VMEM((toks, blocks, out_rows, LANES), jnp.float32),
            pltpu.VMEM((toks, blocks, LANES), jnp.float32),
            pltpu.VMEM((out_rows, EX_DEV, LANES), jnp.float32),
            pltpu.VMEM((feats, out_rows // feats, EX_DEV, LANES), jnp.float32),
            dma((pieces, 4)),
            dma((4,)),
            dma((blocks,)),
            dma((2, blocks)),
            dma((blocks, toks - 1)),
            dma((toks, blocks)),
            dma((toks - 1,)),
            dma((toks,)),
            dma((feats - 1,)),
            dma((feats,)),
        ],
        compiler_params=pltpu.CompilerParams(
            collective_id=0, has_side_effects=True, vmem_limit_bytes=60 * 2**20
        ),
        cost_estimate=pl.CostEstimate(
            flops=2 * rows * R * (in_columns + out_columns),
            bytes_accessed=2 * rows * (in_columns + out_columns),
            transcendentals=0,
        ),
    )(activations, out_grads, proj_in, proj_out, block_example, block_fill)


def solution(mesh):
    in_specs = (
        P(("dom", "tok"), "feat"),
        P(("dom", "tok"), "feat"),
        P(None, "feat"),
        P(None, "feat"),
        P(("dom", "tok")),
        P(("dom", "tok")),
    )
    out_specs = P(("dom", "tok"), "feat")
    body = functools.partial(shards, mesh.shape["feat"], mesh.shape["tok"])
    return jax.shard_map(body, mesh=mesh, in_specs=in_specs, out_specs=out_specs, check_vma=False)
```

time: 44.4 us -> 35.5 us (0.80)
  local copies, waits for them, and re-layouts: 6.04 us -> 1.38 us
  Pallas kernels: 38.1 us -> 33.9 us
    unnamed x11 -> x1, local copies, waits for them, and re-layouts: 6.04 us -> 1.38 us
    pallas_call x1, Pallas kernels: 38.1 us -> 33.9 us  [shards(): pl.pallas_call(functools.partial(kernel, feats, toks, blocks, end_blocks,...]
where the time goes in v2:
time: 35.5 us; the launch traced here: 35.3 us
  Pallas kernels  33.9 us (95%)
  local copies, waits for them, and re-layouts  1.38 us (4%)
    pallas_call x1, Pallas kernels, shards(): pl.pallas_call(functools.partial(kernel, feats, toks, blocks, end_blocks,...  33.9 us
    unnamed x1, local copies, waits for them, and re-layouts  1.38 us

profile of v2, /device:TPU:0, one launch (start us, length us, event | category | flops | bytes accessed | tf_op | source)
XLA Modules:
  0.0 35.3 jit_solution(4455587653340570194)
XLA Ops:
  0.0 33.9 %shard_map.64 = f32[8,1024]{1,0:T(8,128)} custom-call(bf16[2048,3584]{1,0:T(8,128)(2,1)} %act_ref.1, bf16[2048,1024]{1,0:T(8,128)(2,1)} %grad_ref.1, bf16[64,3584]{1,0:T(8,128)(2,1)} %pin_ref.1, bf16[64,1024]{1,0:T(8,128)(2,1)} %pout_ref.1, s32[16]{0:T(128)} %example_hbm.1, s32[16]{0:T(128)} %fill_hbm.1), custom_call_target="tpu_custom_call" | custom-call | flops 1207959552 | bytes 18874368 | tf_op jit(solution)/shard_map/pallas_call | solution.py:277
  33.9 1.4 %copy.8 = f32[8,1024]{1,0:T(8,128)} copy(f32[8,1024]{1,0:T(8,128)} %shard_map.64) | data formatting | bytes 65536

commit v3 on v2

--- a/solution.py
+++ b/solution.py
@@ -13,6 +13,7 @@
 LANES = 128
 NEAR_LAG = 1
 FAR_LAG = 4
+GATHER_LAG = 3
 MID_BLOCKS = 2
 MESH = pl.DeviceIdType.MESH
 
@@ -150,14 +151,14 @@
             hop(near, block_at(near, step)).start()
 
         @pl.when(jnp.logical_and(
+            is_mid, jnp.logical_and(step >= FAR_LAG, step < far_count + FAR_LAG)))
+        def _():
+            forward(far, step - FAR_LAG)
+
+        @pl.when(jnp.logical_and(
             is_mid, jnp.logical_and(step >= NEAR_LAG, step < near_count + NEAR_LAG)))
         def _():
             forward(near, step - NEAR_LAG)
-
-        @pl.when(jnp.logical_and(
-            is_mid, jnp.logical_and(step >= FAR_LAG, step < far_count + FAR_LAG)))
-        def _():
-            forward(far, step - FAR_LAG)
 
     acc[...] = jnp.zeros_like(acc)
     for b in range(blocks):
@@ -224,13 +225,15 @@
     for j in range(1, toks):
         id_arrival(lax.rem(me + j, toks)).wait_recv()
 
-    @pl.loop(0, owned)
+    @pl.loop(0, owned + GATHER_LAG)
     def _(i):
-        outer(i)
-
-    @pl.loop(0, owned)
-    def _(i):
-        gather(i)
+        @pl.when(i < owned)
+        def _():
+            outer(i)
+
+        @pl.when(i >= GATHER_LAG)
+        def _():
+            gather(i - GATHER_LAG)
 
     acc[...] = acc[...] * feature_scale
     for j in range(1, feats):

time: 35.5 us -> 35.3 us (level)
  no operation moved by 1% of the time
where the time goes in v3:
time: 35.3 us; the launch traced here: 35.2 us
  Pallas kernels  33.8 us (96%)
  local copies, waits for them, and re-layouts  1.38 us (4%)
    pallas_call x1, Pallas kernels, shards(): pl.pallas_call(functools.partial(kernel, feats, toks, blocks, end_blocks,...  33.8 us
    unnamed x1, local copies, waits for them, and re-layouts  1.38 us

profile of v3, /device:TPU:0, one launch (start us, length us, event | category | flops | bytes accessed | tf_op | source)
XLA Modules:
  0.0 35.2 jit_solution(9943208635680015447)
XLA Ops:
  0.0 33.8 %shard_map.64 = f32[8,1024]{1,0:T(8,128)} custom-call(bf16[2048,3584]{1,0:T(8,128)(2,1)} %act_ref.1, bf16[2048,1024]{1,0:T(8,128)(2,1)} %grad_ref.1, bf16[64,3584]{1,0:T(8,128)(2,1)} %pin_ref.1, bf16[64,1024]{1,0:T(8,128)(2,1)} %pout_ref.1, s32[16]{0:T(128)} %example_hbm.1, s32[16]{0:T(128)} %fill_hbm.1), custom_call_target="tpu_custom_call" | custom-call | flops 1207959552 | bytes 18874368 | tf_op jit(solution)/shard_map/pallas_call | solution.py:280
  33.8 1.4 %copy.8 = f32[8,1024]{1,0:T(8,128)} copy(f32[8,1024]{1,0:T(8,128)} %shard_map.64) | data formatting | bytes 65536
